TPU v7x, 256 devices: a whole 4x4x8 slice. The times are simulated.
256 devices in a mesh: slab: 32 (over z, y), pencil: 8 (over x, core).
Axes of the slice: x: 4, y: 4, z: 8, core: 2. Of those that a mesh axis runs over, the one named last changes fastest.
Arguments:
- activation: bfloat16 [256, 256, 16, 256], P('pencil', 'slab'), may hold values from -6 to 6
- preact: bfloat16 [256, 256, 16, 256], P('pencil', 'slab'), may hold values from -9 to 9
- cotangent: bfloat16 [256, 256, 16, 256], P('pencil', 'slab'), may hold values from -6 to 6
- local_weight: float32 [16, 16], replicated, may hold values from -1.5 to 1.5
- spectral_weight: float32 [32, 32, 32, 2, 256], P('slab', None, 'pencil'), may hold values from -24 to 24
Outputs:
- grad_activation: bfloat16 [256, 256, 16, 256], P('pencil', 'slab')
- grad_local: float32 [16, 16], replicated
- grad_spectral: float32 [32, 32, 32, 2, 256], P('slab', None, 'pencil')
All inputs are finite; a program needn't handle non-finite values.
Results may differ from a plain program's by a relative error of at most 0.002.
Values sent between devices are 32-bit elements; how exact they have to be, the bound alone decides.
A program may use at most 192 MiB of HBM per device.

v0:
```python
import functools

import jax
import jax.numpy as jnp
import ml_dtypes
import numpy as np
from jax import lax
from jax.experimental import pallas as pl
from jax.experimental.pallas import tpu as pltpu
from jax.sharding import PartitionSpec as P

GRID = 256
CHAN = 16
MODES = 32
SLABS = 32
PENCILS = 8
ROWS = GRID // PENCILS
PLANES = GRID // SLABS
LANES = PLANES * CHAN
HALF = MODES // 2 + 1
XROWS = 40
XPAD = 48
CORES = 2
CHIPS = PENCILS // CORES
FIRST = 9
REST = HALF - FIRST
EDGE = CHIPS * HALF
BLOCK = EDGE + XROWS // 8
PARTS = 8
MODE_ROWS = 512
CHUNK = 8
LOADS = ((0, 4), (4, 8), (8, 16), (16, 24), (24, 32))
PAIR = 2
F32 = jnp.float32
BF16 = jnp.bfloat16


def kept(j):
    return np.where(j < MODES // 2, j, j - MODES)


def y_set(p):
    if p == 0:
        return np.array([0, 1, -1, -16])
    return np.array([2 * p, 2 * p + 1, -2 * p - 1, -2 * p])


def pieces(table):
    high = table.astype(np.float32).astype(ml_dtypes.bfloat16)
    low = (table - high.astype(np.float64)).astype(np.float32).astype(ml_dtypes.bfloat16)
    return high, low


def turn(freq, position):
    angle = 2.0 * np.pi * ((freq * position) % GRID) / GRID
    return np.cos(angle), np.sin(angle)


@functools.cache
def tables():
    made = {}
    cells = np.arange(GRID)

    cosine, sine = turn(np.arange(HALF)[:, None], cells[None, :])
    forward_x = np.zeros((XPAD, GRID))
    forward_x[:HALF], forward_x[HALF : 2 * HALF] = cosine, -sine
    made["xf"] = np.concatenate(pieces(forward_x), axis=0)
    high, low = pieces(forward_x[:XROWS])
    made["xi"] = np.concatenate([high, high, low, np.zeros((8, GRID), high.dtype)], axis=0)

    forward_y = np.zeros((PENCILS, 80, 2, ROWS))
    inverse_y = np.zeros((PENCILS, 2, ROWS, PENCILS, 2, 4))
    extra_y = np.zeros((PENCILS, 2, ROWS, LANES))
    for p in range(PENCILS):
        rows = p * ROWS + np.arange(ROWS)
        for d in range(PENCILS):
            cosine, sine = turn(y_set(d)[:, None], rows[None, :])
            forward_y[p, 8 * d : 8 * d + 4, 0], forward_y[p, 8 * d : 8 * d + 4, 1] = cosine, sine
            forward_y[p, 8 * d + 4 : 8 * d + 8, 0], forward_y[p, 8 * d + 4 : 8 * d + 8, 1] = -sine, cosine
            inverse_y[p, 0, :, d, 0], inverse_y[p, 0, :, d, 1] = cosine.T, -sine.T
            inverse_y[p, 1, :, d, 0], inverse_y[p, 1, :, d, 1] = sine.T, cosine.T
        cosine, sine = turn(16, rows)
        forward_y[p, 64, 0], forward_y[p, 64, 1] = cosine, sine
        forward_y[p, 65, 0], forward_y[p, 65, 1] = -sine, cosine
        extra_y[p, 0], extra_y[p, 1] = cosine[:, None], sine[:, None]
    high, low = pieces(forward_y.reshape(PENCILS, 80, 2 * ROWS))
    made["yf"] = np.concatenate([high, high, low], axis=2)
    high, low = pieces(inverse_y.reshape(PENCILS, 2 * ROWS, 64))
    made["yi"] = np.concatenate([high, high, low], axis=2)
    made["ye"] = extra_y.astype(np.float32)

    z_freq = kept(np.arange(MODES)).reshape(8, 4)
    slab = np.arange(SLABS)
    cosine, sine = turn(z_freq[:, :, None], 8 * slab[None, None, :])
    cosine, sine = cosine[:, :, None, :], sine[:, :, None, :]
    forward_z = np.zeros((8, 4, 4, 2, 2, SLABS, 2, 4))
    for q in range(4):
        forward_z[:, q, :, :, 0, :, 0, q], forward_z[:, q, :, :, 0, :, 1, q] = cosine, sine
        forward_z[:, q, :, :, 1, :, 0, q], forward_z[:, q, :, :, 1, :, 1, q] = -sine, cosine
    forward_z = forward_z.reshape(MODE_ROWS, SLABS, 8)
    kinds = [forward_z]
    for order in ([3, 2, 1, 0], [0, 2, 1, 3]):
        mirrored = np.zeros_like(forward_z)
        for q in range(4):
            mirrored[:, :, order[q]] = forward_z[:, :, q]
            mirrored[:, :, 4 + order[q]] = -forward_z[:, :, 4 + q]
        kinds.append(mirrored)
    kinds = np.stack(kinds).reshape(3, MODE_ROWS, 256)
    made["zf"] = np.stack(pieces(kinds), axis=1)
    made["zi"] = np.stack(pieces(kinds.transpose(0, 2, 1)), axis=1)
    cosine, sine = turn(z_freq[:, :, None], np.arange(PLANES)[None, None, :])
    spread = np.zeros((2, 8, 4, 4, 2, 2, PLANES, CHAN))
    spread[0] = cosine[:, None, :, None, None, :, None]
    spread[1, :, :, :, :, 0] = sine[:, None, :, None, :, None]
    spread[1, :, :, :, :, 1] = -sine[:, None, :, None, :, None]
    made["tw"] = spread.reshape(2, MODE_ROWS // 8, 8, LANES).astype(np.float32)

    same = np.eye(CHAN)
    of_output = np.broadcast_to(same[None, :, :, None], (PLANES, CHAN, CHAN, CHAN)).reshape(LANES, 256)
    of_input = np.broadcast_to(same[None, :, None, :], (PLANES, CHAN, CHAN, CHAN)).reshape(LANES, 256)
    made["eo"] = (np.concatenate([of_output, of_output]) * float(GRID) ** -3).astype(ml_dtypes.bfloat16)
    made["ei"] = np.concatenate([of_input, of_input]).astype(ml_dtypes.bfloat16)
    made["es"] = np.concatenate([of_input.T[:LANES]] * 2).astype(ml_dtypes.bfloat16)
    return made


TABLE_NAMES = ("xf", "yf", "zf", "zi", "tw", "eo", "ei", "es", "yi", "ye", "xi")


def product(a, b):
    return lax.dot_general(a, b, (((1,), (0,)), ((), ())), preferred_element_type=F32)


def product_t(a, b):
    return lax.dot_general(a, b, (((1,), (1,)), ((), ())), preferred_element_type=F32)


def exact_product(a, b, dims):
    return lax.dot_general(a, b, (dims, ((), ())), precision=lax.Precision.HIGHEST, preferred_element_type=F32)


def split(value):
    high = value.astype(BF16)
    return high, (value - high.astype(F32)).astype(BF16)


def stacked(value):
    high, low = split(value)
    return jnp.concatenate([high, low, high], axis=0)


def gelu_slope(value):
    normal_cdf = 0.5 * (1.0 + lax.erf(value * 0.7071067811865476))
    density = jnp.exp(-0.5 * value * value) * 0.3989422804014327
    return normal_cdf + value * density


def parts_swapped(tile):
    even = lax.broadcasted_iota(jnp.int32, tile.shape, 1) % 2 == 0
    return jnp.where(even, pltpu.roll(tile, 7, 1), pltpu.roll(tile, 1, 1))


def to_pencil(src, dst, send, recv, d):
    return pltpu.make_async_remote_copy(
        src_ref=src,
        dst_ref=dst,
        send_sem=send,
        recv_sem=recv,
        device_id={"pencil": d},
        device_id_type=pl.DeviceIdType.MESH,
    )


def to_slab(src, dst, send, recv, d):
    return pltpu.make_async_remote_copy(
        src_ref=src,
        dst_ref=dst,
        send_sem=send,
        recv_sem=recv,
        device_id={"slab": d},
        device_id_type=pl.DeviceIdType.MESH,
    )


def first_tiles(x):
    return pl.ds(x * FIRST, FIRST)


def rest_tiles(x):
    return pl.ds(CHIPS * FIRST + x * REST, REST)


def y_index(p, q):
    if q < 2:
        return 2 * p + q
    if q == 2:
        return 31 - 2 * p
    return jnp.where(p == 0, 16, 32 - 2 * p)


def modes_kernel(
    act_hbm, pre_hbm, cot_hbm, weight_hbm, local_hbm,
    xf_hbm, yf_hbm, zf_hbm, zi_hbm, tw_hbm, eo_hbm, ei_hbm, es_hbm, yi_hbm, ye_hbm, xi_hbm,
    result_hbm, grad_hbm, sum_hbm,
    act, pre, cot, g_high, g_low, local_part, result,
    xf, yf, zf, zi, tw, eo, ei, es, yi, ye, xi,
    field_x, spread_y,
    out1, pair_in, sum1, in1, edge_in, out2, in2,
    weights, weight_parts, low_modes, out3, in3, out4, in4, edge4, grads,
    sums_acc, sums_a, sums_y, sums_z, sums_mine, sums_all, local_ref, mix,
    table_sem, load_sem, store_sem, own_sem,
    psend, precv, send1, recv1, esend, erecv, send2, recv2, wsend, wrecv,
    send3, recv3, send4, recv4, fsend, xsend, xrecv, gsend, grecv,
    asend, arecv, ysend, yrecv, zsend, zrecv,
):
    slab = lax.axis_index("slab")
    pencil = lax.axis_index("pencil")
    core, chip = pencil % CORES, pencil // CORES
    other = chip * CORES + 1 - core

    my_z, my_y = slab // 4, slab % 4

    slab_peers = [
        (slab // 4 + far_z) % 8 * 4 + (slab + far_y) % 4
        for far_z in (4, 3, 5, 2, 6, 1, 7, 0)
        for far_y in (2, 1, 3, 0)
        if far_z or far_y
    ]

    chunks = ROWS // CHUNK
    loads = []
    for c, (start, stop) in enumerate(LOADS):
        rows = pl.ds(start, stop - start)
        loads.append(
            [
                pltpu.make_async_copy(pre_hbm.at[rows], pre.at[rows], load_sem.at[0, c]),
                pltpu.make_async_copy(cot_hbm.at[rows], cot.at[rows], load_sem.at[1, c]),
                pltpu.make_async_copy(act_hbm.at[rows], act.at[rows], load_sem.at[2, c]),
            ]
        )
    kind = jnp.where(slab < 16, 0, jnp.where(pencil == 0, 2, 1))
    sources = (
        (xf_hbm, xf), (yf_hbm.at[pencil], yf), (zf_hbm.at[kind], zf), (zi_hbm.at[kind], zi), (tw_hbm, tw), (eo_hbm, eo), (ei_hbm, ei), (es_hbm, es),
        (yi_hbm.at[pencil], yi), (ye_hbm.at[pencil], ye), (xi_hbm, xi),
        (local_hbm, local_ref),
    )
    fetch = [pltpu.make_async_copy(a, b, table_sem.at[n]) for n, (a, b) in enumerate(sources)]
    by_name = dict(zip(TABLE_NAMES + ("local",), fetch))
    loads[0][0].start()
    loads[0][1].start()
    by_name["xf"].start()
    for load in loads[1:]:
        load[0].start()
        load[1].start()
    by_name["yf"].start()
    for load in loads:
        load[2].start()
    for name in by_name:
        if name not in ("xf", "yf"):
            by_name[name].start()

    barrier = pltpu.get_barrier_semaphore()

    @pl.loop(1, PENCILS)
    def _(j):
        pl.semaphore_signal(
            barrier, inc=1, device_id={"pencil": (pencil + j) % PENCILS}, device_id_type=pl.DeviceIdType.MESH
        )

    @pl.loop(1, SLABS)
    def _(j):
        pl.semaphore_signal(barrier, inc=1, device_id={"slab": (slab + j) % SLABS}, device_id_type=pl.DeviceIdType.MESH)

    def gradient_values(step):
        for r in range(PAIR):
            y = step * PAIR + r
            for part in range(4):
                rows = pl.ds(part * (LANES // 4), LANES // 4)
                g = cot[y, rows].astype(F32) * gelu_slope(pre[y, rows].astype(F32))
                high, low = split(g)
                g_high[y, rows] = high
                g_low[y, rows] = low

    def store_modes(t, step, modes):
        for r in range(PAIR):
            place = (step * PAIR + r) * XROWS
            place = place if isinstance(place, int) else pl.multiple_of(place, 8)
            field_x[t, pl.ds(place, XROWS), :] = modes[:, r * LANES : (r + 1) * LANES]

    def gradient_modes(step):
        rows = pl.ds(step * PAIR, PAIR)
        both = product_t(xf[...], g_high[rows].reshape(PAIR * LANES, GRID))
        more = product_t(xf[:XPAD], g_low[rows].reshape(PAIR * LANES, GRID))
        store_modes(0, step, both[:XROWS] + both[XPAD : XPAD + XROWS] + more[:XROWS])

    for c, (start, stop) in enumerate(LOADS):
        loads[c][0].wait()
        loads[c][1].wait()
        if c == 0:
            by_name["xf"].wait()
            gradient_values(0)

        for step in range(max(start // PAIR, 1), stop // PAIR):
            gradient_modes(step - 1)
            gradient_values(step)

    gradient_modes(ROWS // PAIR - 1)

    def send_rows(t):
        out1[t, 0, BLOCK - 1] = jnp.zeros((8, LANES), F32)
        out1[t, 1, EDGE:BLOCK] = jnp.zeros((BLOCK - EDGE, 8, LANES), F32)
        for half, ks in enumerate((range(FIRST), range(FIRST, HALF))):
            for first in range(ks.start, ks.stop, 2):
                group = range(first, min(first + 2, ks.stop))
                columns = []
                for k in group:
                    real = field_x[t, pl.ds(k, ROWS, stride=XROWS), :]
                    imag = field_x[t, pl.ds(HALF + k, ROWS, stride=XROWS), :]
                    columns.append(jnp.concatenate([real, imag], axis=0))
                both = product(yf[...], stacked(jnp.concatenate(columns, axis=1)))
                for k in group:
                    modes = both[:, (k - first) * LANES : (k - first + 1) * LANES]
                    for d in range(PENCILS):
                        x = d // CORES
                        place = x * FIRST + k if k < FIRST else CHIPS * FIRST + x * REST + k - FIRST
                        out1[t, d % CORES, place] = modes[8 * d : 8 * d + 8]
                    out1[t, 0, EDGE + k // 4, 2 * (k % 4) : 2 * (k % 4) + 2] = modes[64:66]
            pair_copy(t, half).start()

    def pair_copy(t, half):
        tiles = pl.ds(0, CHIPS * FIRST) if half == 0 else pl.ds(CHIPS * FIRST, BLOCK - CHIPS * FIRST)
        return to_pencil(
            out1.at[t, 1 - core, tiles], pair_in.at[t, tiles], psend.at[t], precv.at[t, half], other
        )

    halves = (first_tiles, rest_tiles)
    spans = (pl.ds(0, FIRST), pl.ds(FIRST, REST))

    def x_copy(t, half, to, source):
        return to_pencil(
            sum1.at[t, halves[half](to)], in1.at[t, source, spans[half]], send1.at[t, half], recv1.at[t, source, half],
            to * CORES + core,
        )

    def send_sums(t):
        for half in range(2):
            pair_copy(t, half).wait_recv()
            for j in (2, 1, 3, 0):
                x = (chip + j) % CHIPS
                tiles = halves[half](x)
                sum1[t, tiles] = out1[t, core, tiles] + pair_in[t, tiles]
                if j:
                    x_copy(t, half, x, chip).start()
        sum1[t, EDGE:BLOCK] = out1[t, core, EDGE:BLOCK] + pair_in[t, EDGE:BLOCK]

        @pl.when((core == 0) & (chip != 0))
        def _():
            to_pencil(
                sum1.at[t, pl.ds(EDGE, BLOCK - EDGE)], edge_in.at[t, chip], esend.at[t], erecv.at[t, chip], 0
            ).start()

    by_name["yf"].wait()
    pl.semaphore_wait(barrier, PENCILS - 1 + SLABS - 1)
    send_rows(0)
    send_sums(0)

    @pl.loop(1, PENCILS)
    def _(j):
        d = (pencil + j) % PENCILS
        to_pencil(weight_hbm.at[pl.ds(2 * d, 2)], weights.at[pl.ds(4 * pencil, 2)], wsend, wrecv, d).start()

        @pl.when(d != 0)
        def _():
            to_pencil(
                weight_hbm.at[pl.ds(31 - 2 * d, 2)], weights.at[pl.ds(4 * pencil + 2, 2)], wsend, wrecv, d
            ).start()

        @pl.when(d == 0)
        def _():
            to_pencil(weight_hbm.at[31], weights.at[4 * pencil + 2], wsend, wrecv, d).start()
            to_pencil(weight_hbm.at[16], weights.at[4 * pencil + 3], wsend, wrecv, d).start()

    for q in range(4):
        pltpu.make_async_copy(weight_hbm.at[y_index(pencil, q)], weights.at[4 * pencil + q], own_sem.at[q]).start()

    for c, (start, stop) in enumerate(LOADS):
        loads[c][2].wait()

        @pl.loop(start // PAIR, stop // PAIR, unroll=True)
        def _(step):
            both = product_t(xf[...], act[pl.ds(step * PAIR, PAIR)].reshape(PAIR * LANES, GRID))
            store_modes(1, step, both[:XROWS] + both[XPAD : XPAD + XROWS])

    send_rows(1)
    lane = lax.broadcasted_iota(jnp.int32, (LANES, LANES), 1) // CHAN
    row = lax.broadcasted_iota(jnp.int32, (LANES, LANES), 0) // CHAN

    def send_tiles(t):
        for half, ks in enumerate((range(FIRST), range(FIRST, HALF))):
            total = sum1[t, halves[half](chip)]
            for j in range(1, CHIPS):
                x = (chip + j) % CHIPS
                x_copy(t, half, x, x).wait_recv()
                total = total + in1[t, x, spans[half]]
            for k in ks:
                if k < 16:
                    out2[t, k] = total[k - ks.start]
                if k > 0:
                    out2[t, MODES - k] = total[k - ks.start]

        @pl.when(pencil == 0)
        def _():
            edge = sum1[t, EDGE:BLOCK]
            for x in range(1, CHIPS):
                to_pencil(
                    sum1.at[t, pl.ds(EDGE, BLOCK - EDGE)], edge_in.at[t, x], esend.at[t], erecv.at[t, x], 0
                ).wait_recv()
                edge = edge + edge_in[t, x]
            for k in range(1, HALF):
                r = 2 * (k % 4)
                out2[t, MODES - k, 3:4] = edge[k // 4, r : r + 1]
                out2[t, MODES - k, 7:8] = edge[k // 4, r + 1 : r + 2]

        for d in slab_peers:
            to_slab(out2.at[t, d], in2.at[t, slab], send2.at[t], recv2.at[t], d).start()

        in2[t, slab] = out2[t, slab]

    send_tiles(0)
    send_sums(1)

    sums_acc[...] = jnp.zeros_like(sums_acc)

    @pl.loop(0, ROWS, step=4, unroll=True)
    def _(first):
        left, right = [], []
        for r in range(4):
            left.append(jnp.concatenate([g_high[first + r], g_low[first + r]], axis=0))
            right.append(act[first + r])
        sums_acc[...] += product_t(jnp.concatenate(left, axis=1), jnp.concatenate(right, axis=1))

    full = jnp.where(lane == row, sums_acc[:LANES] + sums_acc[LANES:], 0.0)
    full = jnp.sum(full.reshape(PLANES, CHAN, LANES), axis=0)
    for shift in (CHAN, 2 * CHAN, 4 * CHAN):
        full = full + pltpu.roll(full, shift, 1)
    o_row = lax.broadcasted_iota(jnp.int32, (CHAN, LANES), 0) % 8
    o_lane = lax.broadcasted_iota(jnp.int32, (CHAN, LANES), 1) // CHAN
    full = jnp.where(o_row == o_lane, full, 0.0).reshape(2, 8, LANES)
    full = jnp.sum(full, axis=1, keepdims=True)
    place = lax.broadcasted_iota(jnp.int32, (8, LANES), 0)
    sums_mine[...] = jnp.where(place == 0, full[0], jnp.where(place == 1, full[1], 0.0))

    @pl.loop(1, PENCILS)
    def _(j):
        d = (pencil + j) % PENCILS
        to_pencil(sums_mine, sums_a.at[pencil], asend, arecv.at[pencil], d).start()

    for name in TABLE_NAMES[2:]:
        by_name[name].wait()

    mode_tiles = (MODE_ROWS // 8, 8, LANES)
    place = lax.broadcasted_iota(jnp.int32, mode_tiles, 1)
    first_part = place % 2 == 0
    first_half = place % 4 < 2

    def z_product(table, value):
        high, low = split(value)
        both = product(table[0], jnp.concatenate([high, low], axis=1))
        return both[:, :LANES] + both[:, LANES:] + product(table[1], high)

    def modes_of(t, expand):
        most = pl.ds(0, SLABS - 1)
        to_slab(out2.at[t, most], in2.at[t, most], send2.at[t], recv2.at[t], slab).wait_recv()
        found = z_product(zf, in2[t].reshape(256, LANES)).reshape(mode_tiles)
        found = found * tw[0] + parts_swapped(found) * tw[1]
        high, low = split(found.reshape(MODE_ROWS, LANES))
        wide = product(jnp.concatenate([high, low], axis=1), expand)
        return jnp.where(first_half, wide[:, :LANES].reshape(mode_tiles), wide[:, LANES:].reshape(mode_tiles))

    def both_parts(tile):
        swapped = parts_swapped(tile)
        return jnp.where(first_part, tile, swapped), jnp.where(first_part, swapped, tile)

    to_pencil(
        weight_hbm.at[pl.ds(0, 28)], weights.at[pl.ds(0, 28)], wsend, wrecv, pencil
    ).wait_recv()
    for q in range(4):
        pltpu.make_async_copy(weight_hbm.at[y_index(pencil, q)], weights.at[4 * pencil + q], own_sem.at[q]).wait()
    weight_parts[0], weight_parts[1] = both_parts(weights[...].reshape(mode_tiles))

    lower = modes_of(0, eo[...])
    swapped = parts_swapped(lower)
    turned = jnp.where(first_part, swapped, -swapped)
    low_modes[0] = lower
    low_modes[1] = turned
    high, low = split((weight_parts[0] * lower + weight_parts[1] * turned).reshape(MODE_ROWS, LANES))
    back = product(jnp.concatenate([high, low], axis=1), es[...]).reshape(mode_tiles)
    back = back * tw[0] - parts_swapped(back) * tw[1]
    out3[...] = z_product(zi, back.reshape(MODE_ROWS, LANES)).reshape(SLABS, 8, LANES)

    for d in slab_peers:
        to_slab(out3.at[d], in3.at[slab], send3, recv3, d).start()

    in3[slab] = out3[slab]

    pick = jnp.where(
        lax.broadcasted_iota(jnp.int32, (LANES, CHAN), 0) % CHAN == lax.broadcasted_iota(jnp.int32, (LANES, CHAN), 1),
        1.0,
        0.0,
    )
    by_name["local"].wait()
    mixed = exact_product(pick, local_ref[...], ((1,), (1,)))
    mixed = exact_product(mixed, pick, ((1,), (1,)))
    mix_high, mix_low = split(jnp.where(lane == row, mixed, 0.0))
    mix_rows = jnp.concatenate([mix_high, mix_high], axis=1)
    mix_more = jnp.concatenate([mix_low, jnp.zeros_like(mix_low)], axis=1)
    mix[...] = jnp.concatenate([mix_rows, mix_more], axis=0)

    @pl.loop(0, ROWS, unroll=4)
    def _(y):
        both = product(mix[...], jnp.concatenate([g_high[y], g_low[y]], axis=0))
        local_part[y] = both[:LANES] + both[LANES:]


    sums_a[pencil] = sums_mine[...]
    for j in range(1, PENCILS):
        d = (pencil + j) % PENCILS
        to_pencil(sums_mine, sums_a.at[d], asend, arecv.at[d], d).wait_recv()
    total = jnp.zeros((8, LANES), F32)
    for d in range(PENCILS):
        total = total + sums_a[d]
    sums_y[my_y] = total
    for j in range(1, 4):
        to_slab(sums_y.at[my_y], sums_y.at[my_y], ysend, yrecv, my_z * 4 + (my_y + j) % 4).start()

    send_tiles(1)

    def back_copy(half, p, to, sem):
        return to_pencil(out4.at[spans[half]], in4.at[p, spans[half]], sem, recv4.at[p, half], to)

    to_slab(out3.at[pl.ds(0, SLABS - 1)], in3.at[pl.ds(0, SLABS - 1)], send3, recv3, slab).wait_recv()
    for half, ks in enumerate((range(FIRST), range(FIRST, HALF))):
        for k in ks:
            out4[k] = in3[k] + in3[MODES - k] if 0 < k < 16 else in3[k]

        @pl.when(pencil == 0)
        def _():
            for k in ks:
                for part in range(2):
                    r = 3 + 4 * part
                    if k > 0:
                        edge4[2 * k + part : 2 * k + part + 1] = in3[MODES - k, r : r + 1]
                        out4[k, r : r + 1] = in3[k, r : r + 1] if k < 16 else jnp.zeros((1, LANES), F32)

        for j in (2, 1, 3):
            x = (chip + j) % CHIPS
            back_copy(half, pencil, x * CORES + core, send4.at[half]).start()
        back_copy(half, pencil, other, send4.at[2]).start()

    @pl.when(pencil == 0)
    def _():
        edge4[0:2] = jnp.zeros((2, LANES), F32)
        edge4[34:40] = jnp.zeros((6, LANES), F32)

        @pl.loop(1, PENCILS)
        def _(d):
            to_pencil(edge4, edge4, xsend, xrecv, d).start()

    in4[pencil] = out4[...]

    upper = modes_of(1, ei[...])
    real, imag = both_parts(upper)
    grads[...] = (low_modes[0] * real + low_modes[1] * imag).reshape(MODES, 16, LANES)

    @pl.loop(1, PENCILS)
    def _(j):
        d = (pencil + j) % PENCILS
        to_pencil(grads.at[pl.ds(4 * d, 2)], grad_hbm.at[pl.ds(2 * pencil, 2)], gsend, grecv, d).start()

        @pl.when(pencil != 0)
        def _():
            to_pencil(
                grads.at[pl.ds(4 * d + 2, 2)], grad_hbm.at[pl.ds(31 - 2 * pencil, 2)], gsend, grecv, d
            ).start()

        @pl.when(pencil == 0)
        def _():
            to_pencil(grads.at[4 * d + 2], grad_hbm.at[31], gsend, grecv, d).start()
            to_pencil(grads.at[4 * d + 3], grad_hbm.at[16], gsend, grecv, d).start()

    for q in range(4):
        pltpu.make_async_copy(grads.at[4 * pencil + q], grad_hbm.at[y_index(pencil, q)], own_sem.at[4 + q]).start()

    to_slab(sums_y.at[pl.ds(0, 3)], sums_y.at[pl.ds(0, 3)], ysend, yrecv, slab).wait_recv()
    total = sums_y[0]
    for j in range(1, 4):
        total = total + sums_y[j]
    sums_z[my_z] = total
    for j in range(1, 8):
        to_slab(sums_z.at[my_z], sums_z.at[my_z], zsend, zrecv, (my_z + j) % 8 * 4 + my_y).start()

    for half in range(2):
        for j in (1, 3, 2):
            d = (chip + j) % CHIPS * CORES + core
            back_copy(half, d, d, send4.at[half]).wait_recv()
            to_pencil(
                in4.at[d, spans[half]], in4.at[d, spans[half]], fsend.at[half], recv4.at[d, half], other
            ).start()

    @pl.when(pencil != 0)
    def _():
        to_pencil(edge4, edge4, xsend, xrecv, 0).wait_recv()

    spread_y[pl.ds(2 * HALF * ROWS, (XROWS - 2 * HALF) * ROWS), :] = jnp.zeros(((XROWS - 2 * HALF) * ROWS, LANES), F32)
    for half, ks in enumerate((range(FIRST), range(FIRST, HALF))):
        for x in range(CHIPS):
            back_copy(half, x * CORES + 1 - core, other, send4.at[2]).wait_recv()
        for first in range(ks.start, ks.stop, 2):
            group = range(first, min(first + 2, ks.stop))
            columns = [jnp.concatenate([in4[p, k] for p in range(PENCILS)], axis=0) for k in group]
            both = product(yi[...], stacked(jnp.concatenate(columns, axis=1)))
            for k in group:
                field = both[:, (k - first) * LANES : (k - first + 1) * LANES]
                edge_real, edge_imag = edge4[2 * k : 2 * k + 1], edge4[2 * k + 1 : 2 * k + 2]
                spread_y[k * ROWS : (k + 1) * ROWS] = field[:ROWS] + ye[0] * edge_real - ye[1] * edge_imag
                spread_y[(HALF + k) * ROWS : (HALF + k + 1) * ROWS] = (
                    field[ROWS:] + ye[0] * edge_imag + ye[1] * edge_real
                )

    to_slab(sums_z.at[pl.ds(0, 7)], sums_z.at[pl.ds(0, 7)], zsend, zrecv, slab).wait_recv()
    total = sums_z[0]
    for j in range(1, 8):
        total = total + sums_z[j]
    sums_all[...] = total * float(GRID) ** -1.5
    stores = [pltpu.make_async_copy(sums_all, sum_hbm, store_sem.at[chunks])]
    stores[0].start()

    for c in range(chunks):

        columns = []
        for r in range(CHUNK):
            value = spread_y[pl.ds(c * CHUNK + r, XROWS, stride=ROWS), :]
            high = value.astype(BF16).astype(F32)
            column = jnp.concatenate([high, value - high, high, jnp.zeros((8, LANES), F32)], axis=0)
            columns.append(column.T.astype(BF16))
        fields = product(jnp.concatenate(columns, axis=0), xi[...])
        for r in range(CHUNK):
            y = c * CHUNK + r
            result[y] = (local_part[y] + fields[r * LANES : (r + 1) * LANES]).astype(BF16)

        rows = pl.ds(c * CHUNK, CHUNK)
        stores.append(pltpu.make_async_copy(result.at[rows], result_hbm.at[rows], store_sem.at[c]))
        stores[-1].start()

    to_pencil(weights.at[pl.ds(0, 28)], weights.at[pl.ds(0, 28)], wsend, wrecv, pencil).wait_send()
    for t in range(2):
        to_pencil(out1.at[t, 1 - core], pair_in.at[t], psend.at[t], precv.at[t, 0], other).wait_send()
        for half in range(2):
            some = in1.at[t, pl.ds(0, 3), spans[half]]
            to_pencil(some, some, send1.at[t, half], recv1.at[t, 0, half], other).wait_send()
        most = pl.ds(0, SLABS - 1)
        to_slab(out2.at[t, most], in2.at[t, most], send2.at[t], recv2.at[t], slab).wait_send()

        @pl.when((core == 0) & (chip != 0))
        def _():
            to_pencil(
                sum1.at[t, pl.ds(EDGE, BLOCK - EDGE)], edge_in.at[t, chip], esend.at[t], erecv.at[t, chip], 0
            ).wait_send()

    to_pencil(sums_a.at[pl.ds(0, 7)], sums_a.at[pl.ds(0, 7)], asend, arecv.at[0], pencil).wait_send()
    to_slab(sums_y.at[pl.ds(0, 3)], sums_y.at[pl.ds(0, 3)], ysend, yrecv, slab).wait_send()
    to_slab(sums_z.at[pl.ds(0, 7)], sums_z.at[pl.ds(0, 7)], zsend, zrecv, slab).wait_send()
    to_slab(out3.at[pl.ds(0, 31)], in3.at[pl.ds(0, 31)], send3, recv3, slab).wait_send()
    for half in range(2):
        some = in4.at[pl.ds(0, 3), spans[half]]
        to_pencil(some, some, send4.at[half], recv4.at[0, half], other).wait_send()
        to_pencil(some, some, fsend.at[half], recv4.at[0, half], other).wait_send()
    to_pencil(out4, in4.at[pencil], send4.at[2], recv4.at[pencil, 0], other).wait_send()

    @pl.when(pencil == 0)
    def _():
        for d in range(1, PENCILS):
            to_pencil(edge4, edge4, xsend, xrecv, d).wait_send()

    to_pencil(grads.at[pl.ds(0, 28)], grad_hbm.at[pl.ds(0, 28)], gsend, grecv, pencil).wait()
    for q in range(4):
        pltpu.make_async_copy(grads.at[4 * pencil + q], grad_hbm.at[y_index(pencil, q)], own_sem.at[4 + q]).wait()
    for store in stores:
        store.wait()


def last_kernel(
    result_hbm, grad_in, sum_hbm,
    out_hbm, local_hbm, grad_out,
    result, grad, sum_ref, local_ref, load_sem, store_sem,
):
    rows = [pl.ds(c * (ROWS // PARTS), ROWS // PARTS) for c in range(PARTS)]
    loads = [pltpu.make_async_copy(result_hbm.at[r], result.at[r], load_sem.at[c]) for c, r in enumerate(rows)]
    stores = [pltpu.make_async_copy(result.at[r], out_hbm.at[r], store_sem.at[c]) for c, r in enumerate(rows)]
    loads.append(pltpu.make_async_copy(grad_in, grad, load_sem.at[PARTS]))
    stores.append(pltpu.make_async_copy(grad, grad_out, store_sem.at[PARTS]))
    load_sum = pltpu.make_async_copy(sum_hbm, sum_ref, load_sem.at[PARTS + 1])
    load_sum.start()
    for load in loads:
        load.start()

    o_row = lax.broadcasted_iota(jnp.int32, (CHAN, LANES), 0)
    o_lane = lax.broadcasted_iota(jnp.int32, (CHAN, LANES), 1)
    load_sum.wait()
    total = jnp.where(o_row < 8, sum_ref[0:1], sum_ref[1:2])
    total = jnp.where(o_row % 8 == o_lane // CHAN, total, 0.0)
    pick = jnp.where(
        lax.broadcasted_iota(jnp.int32, (LANES, CHAN), 0) % CHAN == lax.broadcasted_iota(jnp.int32, (LANES, CHAN), 1),
        1.0,
        0.0,
    )
    local_ref[...] = exact_product(total, pick, ((1,), (0,)))
    store_local = pltpu.make_async_copy(local_ref, local_hbm, store_sem.at[PARTS + 1])
    store_local.start()
    for load, store in zip(loads, stores):
        load.wait()
        store.start()
    for store in stores:
        store.wait()
    store_local.wait()


def on_device(activation, preact, cotangent, local_weight, spectral_weight):
    made = tables()
    fields = [a.reshape(ROWS, LANES, GRID) for a in (activation, preact, cotangent)]
    weight = spectral_weight[0].reshape(MODES, 4, 2, 2, LANES).transpose(0, 1, 3, 2, 4).reshape(MODES, 16, LANES)
    any_space = pl.BlockSpec(memory_space=pl.ANY)
    dma = pltpu.SemaphoreType.DMA
    field = pltpu.VMEM((ROWS, LANES, GRID), BF16)
    wide_field = pltpu.VMEM((ROWS, LANES, GRID), F32)
    tile = (8, LANES)
    result, grad, total = pl.pallas_call(
        modes_kernel,
        out_shape=(
            jax.ShapeDtypeStruct((ROWS, LANES, GRID), BF16),
            jax.ShapeDtypeStruct((MODES, 16, LANES), F32),
            jax.ShapeDtypeStruct(tile, F32),
        ),
        in_specs=[any_space] * (5 + len(TABLE_NAMES)),
        out_specs=(any_space, any_space, any_space),
        scratch_shapes=[
            field, field, field, field, field, wide_field, field,
            pltpu.VMEM((2 * XPAD, GRID), BF16),
            pltpu.VMEM((80, 192), BF16),
            pltpu.VMEM((2, MODE_ROWS, 256), BF16),
            pltpu.VMEM((2, 256, MODE_ROWS), BF16),
            pltpu.VMEM((2, MODE_ROWS // 8, 8, LANES), F32),
            pltpu.VMEM((256, 256), BF16),
            pltpu.VMEM((256, 256), BF16),
            pltpu.VMEM((256, LANES), BF16),
            pltpu.VMEM((64, 192), BF16),
            pltpu.VMEM((2, ROWS, LANES), F32),
            pltpu.VMEM((128, GRID), BF16),
            pltpu.VMEM((2, ROWS * XROWS, LANES), F32),
            pltpu.VMEM((ROWS * XROWS, LANES), F32),
            pltpu.VMEM((2, CORES, BLOCK) + tile, F32),
            pltpu.VMEM((2, BLOCK) + tile, F32),
            pltpu.VMEM((2, BLOCK) + tile, F32),
            pltpu.VMEM((2, CHIPS, HALF) + tile, F32),
            pltpu.VMEM((2, CHIPS, BLOCK - EDGE) + tile, F32),
            pltpu.VMEM((2, SLABS) + tile, F32),
            pltpu.VMEM((2, SLABS) + tile, F32),
            pltpu.VMEM((MODES, 16, LANES), F32),
            pltpu.VMEM((2, MODE_ROWS // 8, 8, LANES), F32),
            pltpu.VMEM((2, MODE_ROWS // 8, 8, LANES), F32),
            pltpu.VMEM((SLABS,) + tile, F32),
            pltpu.VMEM((SLABS,) + tile, F32),
            pltpu.VMEM((HALF,) + tile, F32),
            pltpu.VMEM((PENCILS, HALF) + tile, F32),
            pltpu.VMEM((XROWS, LANES), F32),
            pltpu.VMEM((MODES, 16, LANES), F32),
            pltpu.VMEM((2 * LANES, LANES), F32),
            pltpu.VMEM((PENCILS,) + tile, F32),
            pltpu.VMEM((4,) + tile, F32),
            pltpu.VMEM((8,) + tile, F32),
            pltpu.VMEM(tile, F32),
            pltpu.VMEM(tile, F32),
            pltpu.VMEM((CHAN, CHAN), F32),
            pltpu.VMEM((2 * LANES, 2 * LANES), BF16),
            dma((len(TABLE_NAMES) + 1,)), dma((3, len(LOADS))), dma((ROWS // CHUNK + 1,)), dma((8,)),
            dma((2,)), dma((2, 2)), dma((2, 2)), dma((2, CHIPS, 2)), dma((2,)), dma((2, CHIPS)),
            dma((2,)), dma((2,)), dma, dma,
            dma, dma, dma((3,)), dma((PENCILS, 2)), dma((2,)), dma, dma, dma, dma,
            dma, dma((PENCILS,)), dma, dma, dma, dma,
        ],
        compiler_params=pltpu.CompilerParams(
            collective_id=0, has_side_effects=True, vmem_limit_bytes=62 * 1024 * 1024
        ),
        cost_estimate=pl.CostEstimate(flops=3_000_000_000, bytes_accessed=11_000_000, transcendentals=2_000_000),
        name="modes",
    )(*fields, weight, local_weight, *(jnp.asarray(made[name]) for name in TABLE_NAMES))
    out, grad_local, grad_spectral = pl.pallas_call(
        last_kernel,
        out_shape=(
            jax.ShapeDtypeStruct((ROWS, LANES, GRID), BF16),
            jax.ShapeDtypeStruct((CHAN, CHAN), F32),
            jax.ShapeDtypeStruct((MODES, 16, LANES), F32),
        ),
        in_specs=[any_space, any_space, any_space],
        out_specs=(any_space, any_space, any_space),
        scratch_shapes=[
            field,
            pltpu.VMEM((MODES, 16, LANES), F32),
            pltpu.VMEM(tile, F32),
            pltpu.VMEM((CHAN, CHAN), F32),
            dma((PARTS + 2,)), dma((PARTS + 2,)),
        ],
        compiler_params=pltpu.CompilerParams(vmem_limit_bytes=62 * 1024 * 1024),
        cost_estimate=pl.CostEstimate(flops=100_000, bytes_accessed=5_000_000, transcendentals=0),
        name="last",
    )(result, grad, total)
    grad_spectral = grad_spectral.reshape(MODES, 4, 2, 2, LANES).transpose(0, 1, 3, 2, 4).reshape(spectral_weight.shape)
    return out.reshape(activation.shape), grad_local, grad_spectral


def solution(mesh):
    field = P("pencil", "slab", None, None)
    modes = P("slab", None, "pencil", None, None)
    return jax.shard_map(
        on_device,
        mesh=mesh,
        in_specs=(field, field, field, P(), modes),
        out_specs=(field, P(), modes),
        check_vma=False,
    )
```

profile of v0, /device:TPU:1, one launch (start us, length us, event | category | flops | bytes accessed | tf_op | source)
XLA Modules:
  0.0 45.0 jit_solution(17835871379778137885)
XLA Ops:
  0.6 41.9 %modes.1 = (bf16[32,128,256]{2,1,0:T(8,128)(2,1)}, f32[32,16,128]{2,1,0:T(8,128)}, f32[8,128]{1,0:T(8,128)}) custom-call(bf16[32,128,256]{2,1,0:T(8,128)(2,1)} %bitcast.14, bf16[32,128,256]{2,1,0:T(8,128)(2,1)} %bitcast.15, bf16[32,128,256]{2,1,0:T(8,128)(2,1)} %bitcast.16, f32[32,16,128]{2,1,0:T(8,128)} %bitcast.17, f32[16,16]{1,0:T(8,128)} %local_hbm.1, ...), custom_call_target="tpu_custom_call" | custom-call | flops 3000000000 | bytes 11000000 | tf_op jit(solution)/shard_map/modes/pallas_call | solution.py:737
  42.5 2.5 %last.1 = (bf16[32,128,256]{2,1,0:T(8,128)(2,1)}, f32[16,16]{1,0:T(8,128)}, f32[32,16,128]{2,1,0:T(8,128)}) custom-call(bf16[32,128,256]{2,1,0:T(8,128)(2,1)} %get-tuple-element.9.result_hbm, f32[32,16,128]{2,1,0:T(8,128)} %get-tuple-element.10.grad_in, f32[8,128]{1,0:T(8,128)} %get-tuple-element.11.sum_hbm), custom_call_target="tpu_custom_call" | custom-call | flops 100000 | bytes 5000000 | tf_op jit(solution)/shard_map/last/pallas_call | solution.py:797
where the time goes:
time: 45.5 us; the launch traced here: 45 us
  Pallas kernels  44.4 us (98%)
  between operations  0.64 us (1%)
    pallas_call x1, Pallas kernels, on_device(): pl.pallas_call(modes_kernel, out_shape=(jax.ShapeDtypeStruct((ROWS, LANES...  41.9 us
    pallas_call x1, Pallas kernels, on_device(): pl.pallas_call(last_kernel, out_shape=(jax.ShapeDtypeStruct((ROWS, LANES,...  2.52 us

commit v1 on v0

--- a/solution.py
+++ b/solution.py
@@ -271,6 +271,26 @@
     def _(j):
         pl.semaphore_signal(barrier, inc=1, device_id={"slab": (slab + j) % SLABS}, device_id_type=pl.DeviceIdType.MESH)
 
+    def send_weights():
+        @pl.loop(1, PENCILS)
+        def _(j):
+            d = (pencil + j) % PENCILS
+            to_pencil(weight_hbm.at[pl.ds(2 * d, 2)], weights.at[pl.ds(4 * pencil, 2)], wsend, wrecv, d).start()
+
+            @pl.when(d != 0)
+            def _():
+                to_pencil(
+                    weight_hbm.at[pl.ds(31 - 2 * d, 2)], weights.at[pl.ds(4 * pencil + 2, 2)], wsend, wrecv, d
+                ).start()
+
+            @pl.when(d == 0)
+            def _():
+                to_pencil(weight_hbm.at[31], weights.at[4 * pencil + 2], wsend, wrecv, d).start()
+                to_pencil(weight_hbm.at[16], weights.at[4 * pencil + 3], wsend, wrecv, d).start()
+
+        for q in range(4):
+            pltpu.make_async_copy(weight_hbm.at[y_index(pencil, q)], weights.at[4 * pencil + q], own_sem.at[q]).start()
+
     def gradient_values(step):
         for r in range(PAIR):
             y = step * PAIR + r
@@ -303,6 +323,9 @@
         for step in range(max(start // PAIR, 1), stop // PAIR):
             gradient_modes(step - 1)
             gradient_values(step)
+        if c == 2:
+            pl.semaphore_wait(barrier, PENCILS - 1 + SLABS - 1)
+            send_weights()
 
     gradient_modes(ROWS // PAIR - 1)
 
@@ -360,28 +383,8 @@
             ).start()
 
     by_name["yf"].wait()
-    pl.semaphore_wait(barrier, PENCILS - 1 + SLABS - 1)
     send_rows(0)
     send_sums(0)
-
-    @pl.loop(1, PENCILS)
-    def _(j):
-        d = (pencil + j) % PENCILS
-        to_pencil(weight_hbm.at[pl.ds(2 * d, 2)], weights.at[pl.ds(4 * pencil, 2)], wsend, wrecv, d).start()
-
-        @pl.when(d != 0)
-        def _():
-            to_pencil(
-                weight_hbm.at[pl.ds(31 - 2 * d, 2)], weights.at[pl.ds(4 * pencil + 2, 2)], wsend, wrecv, d
-            ).start()
-
-        @pl.when(d == 0)
-        def _():
-            to_pencil(weight_hbm.at[31], weights.at[4 * pencil + 2], wsend, wrecv, d).start()
-            to_pencil(weight_hbm.at[16], weights.at[4 * pencil + 3], wsend, wrecv, d).start()
-
-    for q in range(4):
-        pltpu.make_async_copy(weight_hbm.at[y_index(pencil, q)], weights.at[4 * pencil + q], own_sem.at[q]).start()
 
     for c, (start, stop) in enumerate(LOADS):
         loads[c][2].wait()
@@ -426,8 +429,8 @@
 
         in2[t, slab] = out2[t, slab]
 
+    send_sums(1)
     send_tiles(0)
-    send_sums(1)
 
     sums_acc[...] = jnp.zeros_like(sums_acc)
 
@@ -488,6 +491,8 @@
         pltpu.make_async_copy(weight_hbm.at[y_index(pencil, q)], weights.at[4 * pencil + q], own_sem.at[q]).wait()
     weight_parts[0], weight_parts[1] = both_parts(weights[...].reshape(mode_tiles))
 
+    send_tiles(1)
+
     lower = modes_of(0, eo[...])
     swapped = parts_swapped(lower)
     turned = jnp.where(first_part, swapped, -swapped)
@@ -502,6 +507,73 @@
         to_slab(out3.at[d], in3.at[slab], send3, recv3, d).start()
 
     in3[slab] = out3[slab]
+
+    upper = modes_of(1, ei[...])
+    real, imag = both_parts(upper)
+    grads[...] = (low_modes[0] * real + low_modes[1] * imag).reshape(MODES, 16, LANES)
+
+    @pl.loop(1, PENCILS)
+    def _(j):
+        d = (pencil + j) % PENCILS
+        to_pencil(grads.at[pl.ds(4 * d, 2)], grad_hbm.at[pl.ds(2 * pencil, 2)], gsend, grecv, d).start()
+
+        @pl.when(pencil != 0)
+        def _():
+            to_pencil(
+                grads.at[pl.ds(4 * d + 2, 2)], grad_hbm.at[pl.ds(31 - 2 * pencil, 2)], gsend, grecv, d
+            ).start()
+
+        @pl.when(pencil == 0)
+        def _():
+            to_pencil(grads.at[4 * d + 2], grad_hbm.at[31], gsend, grecv, d).start()
+            to_pencil(grads.at[4 * d + 3], grad_hbm.at[16], gsend, grecv, d).start()
+
+    for q in range(4):
+        pltpu.make_async_copy(grads.at[4 * pencil + q], grad_hbm.at[y_index(pencil, q)], own_sem.at[4 + q]).start()
+
+    sums_a[pencil] = sums_mine[...]
+    for j in range(1, PENCILS):
+        d = (pencil + j) % PENCILS
+        to_pencil(sums_mine, sums_a.at[d], asend, arecv.at[d], d).wait_recv()
+    total = jnp.zeros((8, LANES), F32)
+    for d in range(PENCILS):
+        total = total + sums_a[d]
+    sums_y[my_y] = total
+    for j in range(1, 4):
+        to_slab(sums_y.at[my_y], sums_y.at[my_y], ysend, yrecv, my_z * 4 + (my_y + j) % 4).start()
+
+    def back_copy(half, p, to, sem):
+        return to_pencil(out4.at[spans[half]], in4.at[p, spans[half]], sem, recv4.at[p, half], to)
+
+    to_slab(out3.at[pl.ds(0, SLABS - 1)], in3.at[pl.ds(0, SLABS - 1)], send3, recv3, slab).wait_recv()
+    for half, ks in enumerate((range(FIRST), range(FIRST, HALF))):
+        for k in ks:
+            out4[k] = in3[k] + in3[MODES - k] if 0 < k < 16 else in3[k]
+
+        @pl.when(pencil == 0)
+        def _():
+            for k in ks:
+                for part in range(2):
+                    r = 3 + 4 * part
+                    if k > 0:
+                        edge4[2 * k + part : 2 * k + part + 1] = in3[MODES - k, r : r + 1]
+                        out4[k, r : r + 1] = in3[k, r : r + 1] if k < 16 else jnp.zeros((1, LANES), F32)
+
+        for j in (2, 1, 3):
+            x = (chip + j) % CHIPS
+            back_copy(half, pencil, x * CORES + core, send4.at[half]).start()
+        back_copy(half, pencil, other, send4.at[2]).start()
+
+    @pl.when(pencil == 0)
+    def _():
+        edge4[0:2] = jnp.zeros((2, LANES), F32)
+        edge4[34:40] = jnp.zeros((6, LANES), F32)
+
+        @pl.loop(1, PENCILS)
+        def _(d):
+            to_pencil(edge4, edge4, xsend, xrecv, d).start()
+
+    in4[pencil] = out4[...]
 
     pick = jnp.where(
         lax.broadcasted_iota(jnp.int32, (LANES, CHAN), 0) % CHAN == lax.broadcasted_iota(jnp.int32, (LANES, CHAN), 1),
@@ -520,76 +592,6 @@
     def _(y):
         both = product(mix[...], jnp.concatenate([g_high[y], g_low[y]], axis=0))
         local_part[y] = both[:LANES] + both[LANES:]
-
-
-    sums_a[pencil] = sums_mine[...]
-    for j in range(1, PENCILS):
-        d = (pencil + j) % PENCILS
-        to_pencil(sums_mine, sums_a.at[d], asend, arecv.at[d], d).wait_recv()
-    total = jnp.zeros((8, LANES), F32)
-    for d in range(PENCILS):
-        total = total + sums_a[d]
-    sums_y[my_y] = total
-    for j in range(1, 4):
-        to_slab(sums_y.at[my_y], sums_y.at[my_y], ysend, yrecv, my_z * 4 + (my_y + j) % 4).start()
-
-    send_tiles(1)
-
-    def back_copy(half, p, to, sem):
-        return to_pencil(out4.at[spans[half]], in4.at[p, spans[half]], sem, recv4.at[p, half], to)
-
-    to_slab(out3.at[pl.ds(0, SLABS - 1)], in3.at[pl.ds(0, SLABS - 1)], send3, recv3, slab).wait_recv()
-    for half, ks in enumerate((range(FIRST), range(FIRST, HALF))):
-        for k in ks:
-            out4[k] = in3[k] + in3[MODES - k] if 0 < k < 16 else in3[k]
-
-        @pl.when(pencil == 0)
-        def _():
-            for k in ks:
-                for part in range(2):
-                    r = 3 + 4 * part
-                    if k > 0:
-                        edge4[2 * k + part : 2 * k + part + 1] = in3[MODES - k, r : r + 1]
-                        out4[k, r : r + 1] = in3[k, r : r + 1] if k < 16 else jnp.zeros((1, LANES), F32)
-
-        for j in (2, 1, 3):
-            x = (chip + j) % CHIPS
-            back_copy(half, pencil, x * CORES + core, send4.at[half]).start()
-        back_copy(half, pencil, other, send4.at[2]).start()
-
-    @pl.when(pencil == 0)
-    def _():
-        edge4[0:2] = jnp.zeros((2, LANES), F32)
-        edge4[34:40] = jnp.zeros((6, LANES), F32)
-
-        @pl.loop(1, PENCILS)
-        def _(d):
-            to_pencil(edge4, edge4, xsend, xrecv, d).start()
-
-    in4[pencil] = out4[...]
-
-    upper = modes_of(1, ei[...])
-    real, imag = both_parts(upper)
-    grads[...] = (low_modes[0] * real + low_modes[1] * imag).reshape(MODES, 16, LANES)
-
-    @pl.loop(1, PENCILS)
-    def _(j):
-        d = (pencil + j) % PENCILS
-        to_pencil(grads.at[pl.ds(4 * d, 2)], grad_hbm.at[pl.ds(2 * pencil, 2)], gsend, grecv, d).start()
-
-        @pl.when(pencil != 0)
-        def _():
-            to_pencil(
-                grads.at[pl.ds(4 * d + 2, 2)], grad_hbm.at[pl.ds(31 - 2 * pencil, 2)], gsend, grecv, d
-            ).start()
-
-        @pl.when(pencil == 0)
-        def _():
-            to_pencil(grads.at[4 * d + 2], grad_hbm.at[31], gsend, grecv, d).start()
-            to_pencil(grads.at[4 * d + 3], grad_hbm.at[16], gsend, grecv, d).start()
-
-    for q in range(4):
-        pltpu.make_async_copy(grads.at[4 * pencil + q], grad_hbm.at[y_index(pencil, q)], own_sem.at[4 + q]).start()
 
     to_slab(sums_y.at[pl.ds(0, 3)], sums_y.at[pl.ds(0, 3)], ysend, yrecv, slab).wait_recv()
     total = sums_y[0]

time: 45.5 us -> 46.6 us (1.024)
  Pallas kernels: 44.4 us -> 45.2 us
    pallas_call x1, Pallas kernels: 41.9 us -> 42.6 us  [on_device(): pl.pallas_call(modes_kernel, out_shape=(jax.ShapeDtypeStruct((ROWS, LANES...]
where the time goes in v1:
time: 46.6 us; the launch traced here: 45.8 us
  Pallas kernels  45.2 us (97%)
  between operations  0.64 us (1%)
    pallas_call x1, Pallas kernels, on_device(): pl.pallas_call(modes_kernel, out_shape=(jax.ShapeDtypeStruct((ROWS, LANES...  42.6 us
    pallas_call x1, Pallas kernels, on_device(): pl.pallas_call(last_kernel, out_shape=(jax.ShapeDtypeStruct((ROWS, LANES,...  2.52 us

profile of v1, /device:TPU:1, one launch (start us, length us, event | category | flops | bytes accessed | tf_op | source)
XLA Modules:
  0.0 45.8 jit_solution(17314925530087531165)
XLA Ops:
  0.6 42.6 %modes.1 = (bf16[32,128,256]{2,1,0:T(8,128)(2,1)}, f32[32,16,128]{2,1,0:T(8,128)}, f32[8,128]{1,0:T(8,128)}) custom-call(bf16[32,128,256]{2,1,0:T(8,128)(2,1)} %bitcast.14, bf16[32,128,256]{2,1,0:T(8,128)(2,1)} %bitcast.15, bf16[32,128,256]{2,1,0:T(8,128)(2,1)} %bitcast.16, f32[32,16,128]{2,1,0:T(8,128)} %bitcast.17, f32[16,16]{1,0:T(8,128)} %local_hbm.1, ...), custom_call_target="tpu_custom_call" | custom-call | flops 3000000000 | bytes 11000000 | tf_op jit(solution)/shard_map/modes/pallas_call | solution.py:739
  43.3 2.5 %last.1 = (bf16[32,128,256]{2,1,0:T(8,128)(2,1)}, f32[16,16]{1,0:T(8,128)}, f32[32,16,128]{2,1,0:T(8,128)}) custom-call(bf16[32,128,256]{2,1,0:T(8,128)(2,1)} %get-tuple-element.9.result_hbm, f32[32,16,128]{2,1,0:T(8,128)} %get-tuple-element.10.grad_in, f32[8,128]{1,0:T(8,128)} %get-tuple-element.11.sum_hbm), custom_call_target="tpu_custom_call" | custom-call | flops 100000 | bytes 5000000 | tf_op jit(solution)/shard_map/last/pallas_call | solution.py:799

commit v2 on v0

--- a/solution.py
+++ b/solution.py
@@ -503,6 +503,8 @@
 
     in3[slab] = out3[slab]
 
+    send_tiles(1)
+
     pick = jnp.where(
         lax.broadcasted_iota(jnp.int32, (LANES, CHAN), 0) % CHAN == lax.broadcasted_iota(jnp.int32, (LANES, CHAN), 1),
         1.0,
@@ -532,8 +534,6 @@
     sums_y[my_y] = total
     for j in range(1, 4):
         to_slab(sums_y.at[my_y], sums_y.at[my_y], ysend, yrecv, my_z * 4 + (my_y + j) % 4).start()
-
-    send_tiles(1)
 
     def back_copy(half, p, to, sem):
         return to_pencil(out4.at[spans[half]], in4.at[p, spans[half]], sem, recv4.at[p, half], to)

time: 45.5 us -> 46.6 us (1.024)
  Pallas kernels: 44.4 us -> 45.8 us
    pallas_call x1, Pallas kernels: 41.9 us -> 43.3 us  [on_device(): pl.pallas_call(modes_kernel, out_shape=(jax.ShapeDtypeStruct((ROWS, LANES...]
where the time goes in v2:
time: 46.6 us; the launch traced here: 46.5 us
  Pallas kernels  45.8 us (98%)
  between operations  0.64 us (1%)
    pallas_call x1, Pallas kernels, on_device(): pl.pallas_call(modes_kernel, out_shape=(jax.ShapeDtypeStruct((ROWS, LANES...  43.3 us
    pallas_call x1, Pallas kernels, on_device(): pl.pallas_call(last_kernel, out_shape=(jax.ShapeDtypeStruct((ROWS, LANES,...  2.52 us

profile of v2, /device:TPU:1, one launch (start us, length us, event | category | flops | bytes accessed | tf_op | source)
XLA Modules:
  0.0 46.5 jit_solution(13153532699372543560)
XLA Ops:
  0.6 43.3 %modes.1 = (bf16[32,128,256]{2,1,0:T(8,128)(2,1)}, f32[32,16,128]{2,1,0:T(8,128)}, f32[8,128]{1,0:T(8,128)}) custom-call(bf16[32,128,256]{2,1,0:T(8,128)(2,1)} %bitcast.14, bf16[32,128,256]{2,1,0:T(8,128)(2,1)} %bitcast.15, bf16[32,128,256]{2,1,0:T(8,128)(2,1)} %bitcast.16, f32[32,16,128]{2,1,0:T(8,128)} %bitcast.17, f32[16,16]{1,0:T(8,128)} %local_hbm.1, ...), custom_call_target="tpu_custom_call" | custom-call | flops 3000000000 | bytes 11000000 | tf_op jit(solution)/shard_map/modes/pallas_call | solution.py:737
  43.9 2.5 %last.1 = (bf16[32,128,256]{2,1,0:T(8,128)(2,1)}, f32[16,16]{1,0:T(8,128)}, f32[32,16,128]{2,1,0:T(8,128)}) custom-call(bf16[32,128,256]{2,1,0:T(8,128)(2,1)} %get-tuple-element.9.result_hbm, f32[32,16,128]{2,1,0:T(8,128)} %get-tuple-element.10.grad_in, f32[8,128]{1,0:T(8,128)} %get-tuple-element.11.sum_hbm), custom_call_target="tpu_custom_call" | custom-call | flops 100000 | bytes 5000000 | tf_op jit(solution)/shard_map/last/pallas_call | solution.py:797

commit v3 on v2

--- a/solution.py
+++ b/solution.py
@@ -64,7 +64,11 @@
     cosine, sine = turn(np.arange(HALF)[:, None], cells[None, :])
     forward_x = np.zeros((XPAD, GRID))
     forward_x[:HALF], forward_x[HALF : 2 * HALF] = cosine, -sine
-    made["xf"] = np.concatenate(pieces(forward_x), axis=0)
+    high, low = pieces(forward_x[:XROWS].T)
+    rest = np.zeros((GRID, LANES - 2 * XROWS), high.dtype)
+    for_high = np.concatenate([high, low, rest], axis=1)
+    for_low = np.concatenate([high, np.zeros_like(low), rest], axis=1)
+    made["xf"] = np.concatenate([for_high, for_low], axis=0)
     high, low = pieces(forward_x[:XROWS])
     made["xi"] = np.concatenate([high, high, low, np.zeros((8, GRID), high.dtype)], axis=0)
 
@@ -285,13 +289,13 @@
         for r in range(PAIR):
             place = (step * PAIR + r) * XROWS
             place = place if isinstance(place, int) else pl.multiple_of(place, 8)
-            field_x[t, pl.ds(place, XROWS), :] = modes[:, r * LANES : (r + 1) * LANES]
+            turned = modes[r * LANES : (r + 1) * LANES].T
+            field_x[t, pl.ds(place, XROWS), :] = turned[:XROWS] + turned[XROWS : 2 * XROWS]
 
     def gradient_modes(step):
         rows = pl.ds(step * PAIR, PAIR)
-        both = product_t(xf[...], g_high[rows].reshape(PAIR * LANES, GRID))
-        more = product_t(xf[:XPAD], g_low[rows].reshape(PAIR * LANES, GRID))
-        store_modes(0, step, both[:XROWS] + both[XPAD : XPAD + XROWS] + more[:XROWS])
+        high, low = g_high[rows].reshape(PAIR * LANES, GRID), g_low[rows].reshape(PAIR * LANES, GRID)
+        store_modes(0, step, product(jnp.concatenate([high, low], axis=1), xf[...]))
 
     for c, (start, stop) in enumerate(LOADS):
         loads[c][0].wait()
@@ -388,8 +392,7 @@
 
         @pl.loop(start // PAIR, stop // PAIR, unroll=True)
         def _(step):
-            both = product_t(xf[...], act[pl.ds(step * PAIR, PAIR)].reshape(PAIR * LANES, GRID))
-            store_modes(1, step, both[:XROWS] + both[XPAD : XPAD + XROWS])
+            store_modes(1, step, product(act[pl.ds(step * PAIR, PAIR)].reshape(PAIR * LANES, GRID), xf[:GRID]))
 
     send_rows(1)
     lane = lax.broadcasted_iota(jnp.int32, (LANES, LANES), 1) // CHAN
@@ -745,7 +748,7 @@
         out_specs=(any_space, any_space, any_space),
         scratch_shapes=[
             field, field, field, field, field, wide_field, field,
-            pltpu.VMEM((2 * XPAD, GRID), BF16),
+            pltpu.VMEM((2 * GRID, LANES), BF16),
             pltpu.VMEM((80, 192), BF16),
             pltpu.VMEM((2, MODE_ROWS, 256), BF16),
             pltpu.VMEM((2, 256, MODE_ROWS), BF16),

time: 46.6 us -> 46.6 us (level)
  no operation moved by 1% of the time
where the time goes in v3:
time: 46.6 us; the launch traced here: 46.5 us
  Pallas kernels  45.9 us (98%)
  between operations  0.64 us (1%)
    pallas_call x1, Pallas kernels, on_device(): pl.pallas_call(modes_kernel, out_shape=(jax.ShapeDtypeStruct((ROWS, LANES...  43.3 us
    pallas_call x1, Pallas kernels, on_device(): pl.pallas_call(last_kernel, out_shape=(jax.ShapeDtypeStruct((ROWS, LANES,...  2.52 us

profile of v3, /device:TPU:1, one launch (start us, length us, event | category | flops | bytes accessed | tf_op | source)
XLA Modules:
  0.0 46.5 jit_solution(17104734924517364462)
XLA Ops:
  0.6 43.3 %modes.1 = (bf16[32,128,256]{2,1,0:T(8,128)(2,1)}, f32[32,16,128]{2,1,0:T(8,128)}, f32[8,128]{1,0:T(8,128)}) custom-call(bf16[32,128,256]{2,1,0:T(8,128)(2,1)} %bitcast.14, bf16[32,128,256]{2,1,0:T(8,128)(2,1)} %bitcast.15, bf16[32,128,256]{2,1,0:T(8,128)(2,1)} %bitcast.16, f32[32,16,128]{2,1,0:T(8,128)} %bitcast.17, f32[16,16]{1,0:T(8,128)} %local_hbm.1, ...), custom_call_target="tpu_custom_call" | custom-call | flops 3000000000 | bytes 11000000 | tf_op jit(solution)/shard_map/modes/pallas_call | solution.py:740
  44.0 2.5 %last.1 = (bf16[32,128,256]{2,1,0:T(8,128)(2,1)}, f32[16,16]{1,0:T(8,128)}, f32[32,16,128]{2,1,0:T(8,128)}) custom-call(bf16[32,128,256]{2,1,0:T(8,128)(2,1)} %get-tuple-element.9.result_hbm, f32[32,16,128]{2,1,0:T(8,128)} %get-tuple-element.10.grad_in, f32[8,128]{1,0:T(8,128)} %get-tuple-element.11.sum_hbm), custom_call_target="tpu_custom_call" | custom-call | flops 100000 | bytes 5000000 | tf_op jit(solution)/shard_map/last/pallas_call | solution.py:800
